TPU v7x, 128 devices: a whole 4x4x4 slice. The times are simulated.
128 devices in a mesh: rep: 32 (over y, z_hi, x), shard: 4 (over z_lo, core).
Axes of the slice: x: 4, y: 4, z: 4 (z_hi: 2, z_lo: 2; z = z_hi * 2 + z_lo), core: 2. Of those that a mesh axis runs over, the one named last changes fastest.
Arguments:
- block_input: bfloat16 [16384, 768], P(('rep', 'shard')), may hold values from -6 to 6
- cotangent: float32 [16384, 768], P(('rep', 'shard')), may hold values from -6 to 6
- lengths: int32 [32], P('rep'), may hold values from 257 to 512, as said below
- block_order: int32 [32, 4], P('rep'), may hold values from 0 to 3, as said below
- w_qkv: float32 [768, 3, 768], P(None, None, 'shard'), may hold values from -0.21875 to 0.21875
- w_out: float32 [768, 768], P('shard'), may hold values from -2.5 to 2.5
- w_fc: float32 [768, 3072], P(None, 'shard'), may hold values from -0.21875 to 0.21875
- w_proj: float32 [3072, 768], P('shard'), may hold values from -0.109375 to 0.109375
- mom_qkv: float32 [768, 3, 768], P(None, None, 'shard')
- mom_out: float32 [768, 768], P('shard')
- mom_fc: float32 [768, 3072], P(None, 'shard')
- mom_proj: float32 [3072, 768], P('shard')
- small_params: float32 [12, 768], replicated, as said below
- small_first: float32 [12, 768], replicated, may hold values from -80 to 80
- small_second: float32 [12, 768], replicated, may hold values from 8.192 to 65.536
Outputs:
- block_output: bfloat16 [16384, 768], P(('rep', 'shard'))
- input_grad: float32 [16384, 768], P(('rep', 'shard'))
- grad_qkv: float32 [768, 3, 768], P(None, None, 'shard')
- grad_out: float32 [768, 768], P('shard')
- grad_fc: float32 [768, 3072], P(None, 'shard')
- grad_proj: float32 [3072, 768], P('shard')
- grad_small: float32 [12, 768], replicated
- new_qkv: float32 [768, 3, 768], P(None, None, 'shard')
- new_out: float32 [768, 768], P('shard')
- new_fc: float32 [768, 3072], P(None, 'shard')
- new_proj: float32 [3072, 768], P('shard')
- next_mom_qkv: float32 [768, 3, 768], P(None, None, 'shard')
- next_mom_out: float32 [768, 768], P('shard')
- next_mom_fc: float32 [768, 3072], P(None, 'shard')
- next_mom_proj: float32 [3072, 768], P('shard')
- next_first: float32 [12, 768], replicated
- next_second: float32 [12, 768], replicated
- next_small: float32 [12, 768], replicated
- grad_last_bias: float32 [768], replicated
Inputs may be any that keep to these rules, and one draw needn't show every extreme that they name: `lengths`: each group's sequence length; in every draw one group's is 512 and another's is 257. `block_order`: each row names every block number once; slot 0 holds block 0 and the last slot holds block 1. `small_params`: rows 0 and 2 are positive.
All inputs are finite; a program needn't handle non-finite values.
Results may differ from a plain program's by a relative error of at most 0.023.
Values may be sent and summed in bfloat16 or wider, within the bound.
A program may use at most 256 MiB of HBM per device.

v0:
```python
import math

import jax
import jax.numpy as jnp
from jax import lax
from jax.experimental import pallas as pl
from jax.experimental.pallas import tpu as pltpu
from jax.sharding import PartitionSpec as P

D = 768
HD = 64
FF = 3072
BLOCK = 128
STEP = 10
momentum_decay = 0.95
muon_rate = 0.15
out_rate = 0.75
muon_decay = 0.01
adam_rate = 0.4
beta_one = 0.9
beta_two = 0.999
adam_eps = 1e-08
norm_eps = 1e-05
poly_a = 3.4445
poly_b = -4.775
poly_c = 2.0315
masked_score = -1e30
bf16 = jnp.bfloat16
f32 = jnp.float32


def dot(left, right, dims=((1,), (0,))):
    return lax.dot_general(left, right, (dims, ((), ())), preferred_element_type=f32)


MESH = pl.DeviceIdType.MESH
HALF = 384
SENDS = 40
RECVS = 151


def place():
    rep = lax.axis_index("rep")
    return rep % 4, rep // 8, (rep // 4) % 2, lax.axis_index("shard")


def device(x, y, z, shard):
    return ((y * 2 + z) * 4 + x, shard)


class GroupSum:
    def __init__(self, sides, across, copy, here, total_rows, parts, out, got_one, got_two, got_z, pass_one, pass_two, mid):
        self.sides, self.across, self.copy, self.here = sides, across, copy, here
        self.parts, self.out, self.got, self.got_z = parts, out, (got_one, got_two), got_z
        self.passing, self.mid, self.ends = (pass_one, pass_two), mid, pass_two
        self.big, self.little = total_rows // 4, total_rows // 16
        self.cuts = (self.big // 2, (self.little // 2 + 15) // 16 * 16)

    @staticmethod
    def rows(start, size):
        return pl.ds(pl.multiple_of(start, 16), size)

    def reduce_start(self, step, ref, axis, k):
        p, left, right, over = self.sides[axis]
        n, cut, got = (self.big, self.little)[step], self.cuts[step], self.got[step].at[k]
        opp, nxt, prv = (p + 2) % 4, (p + 1) % 4, (p + 3) % 4
        rows, copy = self.rows, self.copy
        if step == 1:
            direct = [copy(ref.at[rows(c * n, n), :], got.at[i], target) for i, (c, target) in enumerate(((nxt, right), (prv, left), (opp, over)))]
            return direct, (p, ref, n, got)
        first = (
            copy(ref.at[rows(opp * n, cut), :], got.at[0, 0:cut, :], right),
            copy(ref.at[rows(opp * n + cut, n - cut), :], got.at[0, cut:n, :], left),
            copy(ref.at[rows(nxt * n + cut, n - cut), :], got.at[1, cut:n, :], right),
            copy(ref.at[rows(prv * n, cut), :], got.at[1, 0:cut, :], left),
        )
        return first, (p, left, right, nxt, prv, ref, n, cut, got, self.passing[step].at[k])

    def reduce_pass(self, state):
        first, (p, left, right, nxt, prv, ref, n, cut, got, passing) = state
        rows = self.rows
        first[0].wait_recv()
        passing[0:cut, :] = (ref[rows(nxt * n, cut), :].astype(f32) + got[0, 0:cut, :].astype(f32)).astype(bf16)
        second = [self.copy(passing.at[0:cut, :], got.at[2, 0:cut, :], right)]
        first[1].wait_recv()
        passing[cut:n, :] = (ref[rows(prv * n + cut, n - cut), :].astype(f32) + got[0, cut:n, :].astype(f32)).astype(bf16)
        second.append(self.copy(passing.at[cut:n, :], got.at[2, cut:n, :], left))
        return second

    def reduce_end_direct(self, state, dst):
        copies, (p, ref, n, got) = state
        for c in copies:
            c.wait_recv()
        dst[...] = (ref[self.rows(p * n, n), :].astype(f32) + got[0].astype(f32) + got[1].astype(f32) + got[2].astype(f32)).astype(bf16)
        for c in copies:
            c.wait_send()

    def reduce_end(self, state, second, dst):
        first, (p, left, right, nxt, prv, ref, n, cut, got, passing) = state
        for c in (first[2], first[3], *second):
            c.wait_recv()
        dst[...] = (ref[self.rows(p * n, n), :].astype(f32) + got[1].astype(f32) + got[2].astype(f32)).astype(bf16)
        for c in (*first, *second):
            c.wait_send()

    def gather_start(self, step, ref, axis, base):
        p, left, right, over = self.sides[axis]
        n, cut = (self.big, self.little)[step], self.cuts[step]

        def send(chunk, head, target):
            spot = self.rows(base + chunk * n + (0 if head else cut), cut if head else n - cut)
            return self.copy(ref.at[spot, :], ref.at[spot, :], target)

        if step == 1:
            spot = self.rows(base + p * n, n)
            return [self.copy(ref.at[spot, :], ref.at[spot, :], target) for target in (right, left, over)]
        return (send(p, True, right), send(p, False, left), send(p, False, right), send(p, True, left)), (p, left, right, send)

    def gather_pass(self, state):
        first, (p, left, right, send) = state
        first[0].wait_recv()
        second = [send((p + 3) % 4, True, right)]
        first[1].wait_recv()
        second.append(send((p + 1) % 4, False, left))
        return second

    def gather_end(self, state, second):
        for c in (*state[0][2:], *second):
            c.wait_recv()
        for c in (*state[0], *second):
            c.wait_send()

    def one_start(self):
        self.state = [self.reduce_start(0, self.parts.at[k], "xy"[k], k) for k in range(2)]

    def one_pass(self):
        self.second = [self.reduce_pass(state) for state in self.state]

    def two_start(self):
        for k in range(2):
            self.reduce_end(self.state[k], self.second[k], self.mid.at[k])
        self.state = [self.reduce_start(1, self.mid.at[k], "yx"[k], k) for k in range(2)]

    def z_start(self):
        for k in range(2):
            self.reduce_end_direct(self.state[k], self.ends.at[2 + k])
        self.over = [self.copy(self.ends.at[2 + k], self.got_z.at[k], self.across) for k in range(2)]

    def back_start(self):
        x, y = self.here
        self.state = []
        for k in range(2):
            base = (x, y)[k] * self.big
            at = base + (y, x)[k] * self.little
            self.over[k].wait()
            self.out[k, self.rows(at, self.little), :] = (self.ends[2 + k].astype(f32) + self.got_z[k].astype(f32)).astype(bf16)
            self.state.append(self.gather_start(1, self.out.at[k], "yx"[k], base))

    def last_start(self):
        for c in (*self.state[0], *self.state[1]):
            c.wait()
        self.state = [self.gather_start(0, self.out.at[k], "xy"[k], 0) for k in range(2)]

    def last_pass(self):
        self.second = [self.gather_pass(state) for state in self.state]

    def last_end(self):
        for k in range(2):
            self.gather_end(self.state[k], self.second[k])


def sum_scratch(total_rows):
    big, little = total_rows // 4, total_rows // 16
    return [
        pltpu.VMEM((2, 3, big, HALF), bf16),
        pltpu.VMEM((2, 3, little, HALF), bf16),
        pltpu.VMEM((2, little, HALF), bf16),
        pltpu.VMEM((2, big, HALF), bf16),
        pltpu.VMEM((4, little, HALF), bf16),
        pltpu.VMEM((2, big, HALF), bf16),
    ]


def make_gather(sides, copy):
    def start(axis, ref, base, n, cut, unit):
        p, left, right, over = sides[axis]

        def rows(chunk, first):
            at = base + chunk * n + (0 if first else cut)
            return pl.ds(pl.multiple_of(at, unit), cut if first else n - cut)

        def send(chunk, first, target):
            spot = rows(chunk, first)
            return copy(ref.at[spot, :], ref.at[spot, :], target)

        first = (send(p, True, right), send(p, False, left), send(p, False, right), send(p, True, left))
        return first, (p, left, right, send)

    def start_direct(axis, ref, base, n, unit):
        p, *targets = sides[axis]
        spot = pl.ds(pl.multiple_of(base + p * n, unit), n)
        return [copy(ref.at[spot, :], ref.at[spot, :], target) for target in targets]

    def onward(state):
        first, (p, left, right, send) = state
        first[0].wait_recv()
        second = [send((p + 3) % 4, True, right)]
        first[1].wait_recv()
        second.append(send((p + 1) % 4, False, left))
        return second

    def end(state, second):
        for c in (*state[0][2:], *second):
            c.wait_recv()
        for c in (*state[0], *second):
            c.wait_send()

    def both(refs, orders, base, sizes, unit):
        n, cut = sizes[0]
        direct = [c for k in range(2) for c in start_direct(orders[k][0], refs[k], base[k], n, unit)]
        for c in direct:
            c.wait()
        n, cut = sizes[1]
        states = [start(orders[k][1], refs[k], 0, n, cut, unit) for k in range(2)]
        seconds = [onward(state) for state in states]
        for state, second in zip(states, seconds):
            end(state, second)

    return both


def orth_factors(here, sides, sibling, over_z, over_z_next, copy, at, piece, got, halves, gram, gram_low, poly, factor_low, q_all, small_step):
    x, y, z, shard = here
    gather = make_gather(sides, copy)
    n = D // 16
    sib, par = shard + 1 - 2 * (shard % 2), (shard + 2) % 4
    ps = (sib + 2) % 4
    sums = [copy(piece.at[sib], got.at[0], sibling)]
    for k in range(2):
        sums.append(copy(piece.at[par, k], got.at[1, k], over_z[k]))
        sums.append(copy(piece.at[ps, k], got.at[2, k], over_z_next[k]))
    for c in sums:
        c.wait_recv()
    for k in range(2):
        halves[k, pl.ds(at[k], n), :] = piece[shard, k] + got[0, k] + got[1, k] + got[2, k]
    orders = (("y", "x"), ("x", "y"))
    base = (x * 4 * n, y * 4 * n)
    gather([halves.at[0], halves.at[1]], orders, base, ((n, 24), (4 * n, 2 * n)), 8)
    for c in sums:
        c.wait_send()

    tile = 256
    blocks = D // tile

    def eye(r, width, first):
        return (lax.broadcasted_iota(jnp.int32, (tile, width), 0) + r * tile == lax.broadcasted_iota(jnp.int32, (tile, width), 1) + first).astype(f32)

    trace = jnp.zeros((1, 1), f32)
    for r in range(blocks):
        for k in range(2):
            part = halves[k, r * tile : (r + 1) * tile, :] * eye(r, HALF, k * HALF)
            trace = trace + jnp.sum(jnp.sum(part, axis=1, keepdims=True), axis=0, keepdims=True)
    inv = 1.0 / (jnp.sqrt(trace) + 1e-07)
    for r in range(blocks):
        spot = slice(r * tile, (r + 1) * tile)
        for k in range(2):
            cols = slice(k * HALF, k * HALF + HALF)
            g = halves[k, spot, :] * (inv * inv)
            gram[spot, cols] = g
            gram_low[0][spot, cols] = g.astype(bf16)

    for k in range(4):
        small_step()
        now, later = k % 2, (k + 1) % 2

        def poly_rows(r):
            spot = slice(r * tile, (r + 1) * tile)
            poly[spot, :] = (poly_b * gram[spot, :] + poly_c * dot(gram_low[now][spot, :], gram_low[now][...])).astype(bf16)

        def update_rows(r):
            spot = slice(r * tile, (r + 1) * tile)
            p = poly[spot, :]
            if k == 0:
                q = p.astype(f32) + poly_a * eye(r, D, 0)
            else:
                q = poly_a * jnp.concatenate([halves[0, spot, :], halves[1, spot, :]], 1) + dot(p, factor_low[now][...])
            halves[0, spot, :] = q[:, :HALF]
            halves[1, spot, :] = q[:, HALF:]
            if k < 3:
                factor_low[later][spot, :] = q.astype(bf16)
                t = poly_a * gram[spot, :] + dot(p, gram_low[now][...])
                g = poly_a * t + dot(t.astype(bf16), poly[...])
                gram[spot, :] = g
                gram_low[later][spot, :] = g.astype(bf16)

        for r in range(blocks):
            poly_rows(r)
        for r in range(blocks):
            update_rows(r)
    small_step()
    q_all[shard, 0] = (halves[0, 0:HALF, :] * inv).astype(bf16)
    q_all[shard, 1] = (halves[1, 0:HALF, :] * inv).astype(bf16)
    q_all[shard, 2] = (halves[1, HALF:D, :] * inv).astype(bf16)
    top, low_part = pl.ds(0, HALF // 2), pl.ds(HALF // 2, HALF // 2)
    cross = []
    for k in range(2):
        for block, spot in ((1, (top, low_part)[k]), (2 * k, pl.ds(0, HALF))):
            view = q_all.at[shard, block, spot, :]
            cross.append((copy(view, view, over_z[k]), block, spot))
    near = copy(q_all.at[shard], q_all.at[shard], sibling)
    away = (shard + 2) % 4
    onward = []
    for c, block, spot in (cross[0], cross[2], cross[1], cross[3]):
        c.wait_recv()
        view = q_all.at[away, block, spot, :]
        onward.append(copy(view, view, sibling))
    near.wait_recv()
    for c in onward:
        c.wait_recv()
    for c in (*[c for c, block, spot in cross], near, *onward):
        c.wait_send()


def block_kernel(
    x_ref, cot_ref, length_ref, order_ref, wq_hbm, wo_hbm, wf_hbm, wp_hbm, mq_hbm, mo_hbm, mf_hbm, mp_hbm, small_ref,
    out_ref, dx_ref, sums_one, sums_two, small_out, q_all, u_fc, momq, wo32, wf32, wp32, wf_held, wp_held,
    tokens, mixed, probs, bias, head_out, terms, got, passing, wq, wo, wf, wp,
    gact, act, gpre, gheads, gmixed, xhat1, xhat2, resid, gres, parts_one, parts_two, *rest,
):
    one_refs, two_refs = rest[:6], rest[6:12]
    small, qkv_bias, row_place, uq, piece, gram_got, halves, gram, poly = rest[12:21]
    small_got, send, recv, local = rest[21:]
    group = 4 * BLOCK
    nrm, mlow, nrm2, branch = (tokens.at[pl.ds(k * group, group), :] for k in range(4))
    part = [terms.at[pl.ds(k * group, group), :] for k in range(4)]
    gram_low, factor_low = ([ref.at[pl.ds(k * D, D), :] for k in range(2)] for ref in (tokens, terms))
    x, y, z, shard = place()
    sib = shard + 1 - 2 * (shard % 2)
    par = (shard + 2) % 4
    sibling, partner = device(x, y, z, sib), device(x, y, z, par)
    sides = {
        "x": (x, *[device((x + d) % 4, y, z, shard) for d in (3, 1, 2)]),
        "y": (y, *[device(x, (y + d) % 4, z, shard) for d in (3, 1, 2)]),
    }
    across = device(x, y, 1 - z, shard)
    far_sib = (sib + 2) % 4
    partners = (sibling, partner, device(x, y, z, far_sib), device(x, y, 1 - z, par), device(x, y, 1 - z, far_sib), *sides["x"][1:], *sides["y"][1:], across)
    barrier = pltpu.get_barrier_semaphore()
    for other in partners:
        pl.semaphore_signal(barrier, inc=1, device_id=other, device_id_type=MESH)
    loads = [pltpu.make_async_copy(src, dst, local.at[k]) for k, (src, dst) in enumerate(((wq_hbm, momq), (wo_hbm, wo32), (wf_hbm, wf32), (wp_hbm, wp32)))]
    for load in loads:
        load.start()

    rows = BLOCK

    def chunk(index, size=rows, at=0):
        return pl.ds(pl.multiple_of(index * rows + at, 16), size)

    own, own_sib, own_par, own_ps = chunk(shard), chunk(sib), chunk(par), chunk((sib + 2) % 4)
    near = pl.multiple_of((shard // 2) * 256, 256)
    far = pl.multiple_of(256 - near, 256)
    used = [0]

    free = list(range(SENDS))

    class Copy:
        def __init__(self, src, dst, target):
            self.slot = free.pop(0)
            self.copy = pltpu.make_async_remote_copy(
                src_ref=src, dst_ref=dst, send_sem=send.at[self.slot], recv_sem=recv.at[used[0]], device_id=target, device_id_type=MESH
            )
            used[0] += 1
            self.copy.start()

        def wait_recv(self):
            self.copy.wait_recv()

        def wait_send(self):
            self.copy.wait_send()
            free.append(self.slot)

        def wait(self):
            self.wait_recv()
            self.wait_send()

    copy = Copy
    sum_one = GroupSum(sides, across, copy, (x, y), 2 * D, parts_one, sums_one, *one_refs)
    sum_two = GroupSum(sides, across, copy, (x, y), D, parts_two, sums_two, *two_refs)
    steps = [
        sibling,
        partner,
        across,
        device(x + 1 - 2 * (x % 2), y, z, shard),
        device(3 - x, y, z, shard),
        device(x, y + 1 - 2 * (y % 2), z, shard),
        device(x, 3 - y, z, shard),
    ]
    small_copies = []

    def small_step():
        k = len(small_copies)
        if k > 0:
            small_copies[-1].wait()
            small_out[...] += small_got[k - 1]
        if k < len(steps):
            small_copies.append(copy(small_out, small_got.at[k], steps[k]))

    one_way, both_ways = (partner, partner), (partner, device(x, y, 1 - z, par))

    class Spread:
        def __init__(self, ref, ways):
            self.ref = ref
            self.cross = [self.to(shard, 64 * i, ways[i]) for i in range(2)]
            self.direct = copy(ref.at[own, :], ref.at[own, :], sibling)

        def to(self, index, at, target):
            spot = chunk(index, 64, at)
            return copy(self.ref.at[spot, :], self.ref.at[spot, :], target)

        def near(self):
            self.direct.wait_recv()

        def far(self):
            onward = []
            for i in range(2):
                self.cross[i].wait_recv()
                onward.append(self.to(par, 64 * i, sibling))
            for c in onward:
                c.wait_recv()
            for c in (*self.cross, self.direct, *onward):
                c.wait_send()

    class Fold:
        def __init__(self, k, ways):
            self.k, self.ways = k, ways

        def start_far(self):
            self.a = copy(part[self.k].at[own_ps, :], got.at[self.k, 0], sibling)

        def start_near(self):
            self.b = copy(part[self.k].at[own_sib, :], got.at[self.k, 1], sibling)

        def cross(self):
            self.a.wait_recv()
            passing[self.k] = (part[self.k][own_par, :].astype(f32) + got[self.k, 0].astype(f32)).astype(bf16)
            halves = (pl.ds(0, 64), pl.ds(64, 64))
            self.c = [copy(passing.at[self.k, spot, :], got.at[self.k, 2, spot, :], way) for spot, way in zip(halves, self.ways)]

        def end(self):
            self.b.wait_recv()
            for c in self.c:
                c.wait_recv()
            for c in (self.a, self.b, *self.c):
                c.wait_send()
            return part[self.k][own, :].astype(f32) + got[self.k, 1].astype(f32) + got[self.k, 2].astype(f32)

    def norm(v):
        centred = v - jnp.mean(v, axis=-1, keepdims=True)
        r = lax.rsqrt(jnp.mean(centred * centred, axis=-1, keepdims=True) + norm_eps)
        return centred * r, r

    def norm_grad(xhat, r, gain, c):
        cg = c * gain
        return r * (cg - jnp.mean(cg, -1, keepdims=True) - xhat * jnp.mean(cg * xhat, -1, keepdims=True))

    def total(v):
        return jnp.sum(v, axis=0, keepdims=True)

    nt, tn = ((1,), (1,)), ((0,), (0,))
    hc = wq.shape[0] // 3
    heads = hc // HD
    scale = HD ** -0.5

    small[...] = small_ref[...].astype(bf16).astype(f32)
    length = length_ref[0]

    def places(slot, axis):
        return lax.broadcasted_iota(jnp.int32, (rows, 1) if axis == 0 else (1, rows), axis) + order_ref[0, slot] * rows

    live = (places(shard, 0) < length).astype(f32)
    xf = x_ref[...].astype(f32)
    hat, r_one = norm(xf)
    xhat1[...] = hat
    nrm[own, :] = (hat * small[0:1, :] + small[1:2, :]).astype(bf16)
    mlow[own, :] = (cot_ref[...] * live).astype(bf16)
    pl.semaphore_wait(barrier, len(partners))
    go_nrm = Spread(nrm, one_way)
    go_mlow = Spread(mlow, both_ways)
    for slot in range(4):
        row_place[:, slot * rows : (slot + 1) * rows] = places(slot, 1)
    row = row_place[...]
    for slot in range(4):
        bias[slot * rows : (slot + 1) * rows, :] = jnp.where((row <= places(slot, 0)) & (row < length), 0.0, masked_score)
    for part_of, line in ((0, 4), (2, 5)):
        mine = jnp.zeros((1, hc), f32)
        for s in range(4):
            mine = jnp.where(shard == s, small[line : line + 1, s * hc : (s + 1) * hc], mine)
        qkv_bias[:, part_of * hc : (part_of + 1) * hc] = mine
    qkv_bias[:, hc : 2 * hc] = jnp.zeros((1, hc), f32)
    fc_bias = small[pl.ds(7 + shard, 1), :]
    loads[0].wait()
    wq[...] = momq[...].astype(bf16)
    loads[1].wait()
    wo[...] = wo32[...].astype(bf16)

    def mix(at):
        spot = pl.ds(at, 256)
        mixed[spot, :] = (dot(nrm[spot, :], wq[...], nt) + qkv_bias[...]).astype(bf16)

    go_nrm.near()
    mix(near)
    go_nrm.far()
    mix(far)

    def head(h, part_of):
        lo = part_of * hc + h * HD
        return slice(lo, lo + HD)

    for h in range(heads):

        def attend(i):
            spot = slice(i * 256, i * 256 + 256)
            s = dot(mixed[spot, head(h, 0)], mixed[:, head(h, 1)], nt) * scale + bias[spot, :]
            e = jnp.exp(s - jnp.max(s, axis=-1, keepdims=True))
            p = (e * (1.0 / jnp.sum(e, axis=-1, keepdims=True))).astype(bf16)
            probs[h, spot, :] = p
            head_out[spot, head(h, 0)] = dot(p, mixed[:, head(h, 2)]).astype(bf16)

        for i in range(2):
            attend(i)

    fold = Fold(0, one_way)
    part[0][pl.ds(far, 256), :] = dot(head_out[pl.ds(far, 256), :], wo[...]).astype(bf16)
    fold.start_far()
    part[0][pl.ds(near, 256), :] = dot(head_out[pl.ds(near, 256), :], wo[...]).astype(bf16)
    fold.start_near()
    fold.cross()
    go_mlow.near()
    go_mlow.far()
    loads[2].wait()
    wf[...] = wf32[...].astype(bf16)
    loads[3].wait()
    wp[...] = wp32[...].astype(bf16)

    mom_loads = [pltpu.make_async_copy(src, dst, local.at[4 + k]) for k, (src, dst) in enumerate(((mo_hbm, wo32), (mf_hbm, wf32), (mp_hbm, wp32), (mq_hbm, momq), (wf_hbm, wf_held), (wp_hbm, wp_held)))]
    for load in mom_loads:
        load.start()

    def activation_grad(i):
        spot = slice(i * 256, i * 256 + 256)
        gact[spot, :] = dot(mlow[spot, :], wp[...], nt)

    for i in range(2):
        activation_grad(i)
    res = x_ref[...].astype(f32) + fold.end() + small[6:7, :]
    resid[...] = res
    hat, r_two = norm(res)
    xhat2[...] = hat
    nrm2[own, :] = (hat * small[2:3, :] + small[3:4, :]).astype(bf16)
    go_nrm2 = Spread(nrm2, both_ways)

    def feed(at):
        spot = pl.ds(at, 256)
        hidden = dot(nrm2[spot, :], wf[...]) + fc_bias
        k = 0.7978845608028654
        square = hidden * hidden
        t = jnp.tanh(k * (hidden + 0.044715 * hidden * square))
        half = 0.5 * (1.0 + t)
        act[spot, :] = (hidden * half).astype(bf16)
        slope = half + 0.5 * hidden * (1.0 - t * t) * (k + (3 * 0.044715 * k) * square)
        gpre[spot, :] = (slope * gact[spot, :]).astype(bf16)

    go_nrm2.near()
    feed(near)
    go_nrm2.far()
    feed(far)
    fold = Fold(1, both_ways)
    part[1][pl.ds(far, 256), :] = dot(gpre[pl.ds(far, 256), :], wf[...], nt).astype(bf16)
    fold.start_far()
    part[1][pl.ds(near, 256), :] = dot(gpre[pl.ds(near, 256), :], wf[...], nt).astype(bf16)
    fold.start_near()
    fold.cross()

    def grad_columns(parts, base, left, right, width):
        for c in range(left.shape[1] // width):
            value = dot(left[:, c * width : (c + 1) * width], right[...], tn).astype(bf16)
            spot = pl.ds(base + c * width, width)
            parts[0, spot, :] = value[:, :HALF]
            parts[1, spot, :] = value[:, HALF:]

    grad_columns(parts_one, 0, nrm2, gpre, 256)
    grad_columns(parts_one, D, act, mlow, 256)
    sum_one.one_start()
    small_out[11:12, :] = total(mlow[own, :].astype(f32))
    c_two = fold.end()
    hat = xhat2[...]
    small_out[2:3, :] = total(c_two * hat)
    small_out[3:4, :] = total(c_two)
    g = cot_ref[...] * live + norm_grad(hat, r_two, small[2:3, :], c_two)
    gres[...] = g
    branch[own, :] = g.astype(bf16)
    go_branch = Spread(branch, one_way)
    sum_one.one_pass()
    small_out[6:7, :] = total(branch[own, :].astype(f32))
    pre_sum = total(gpre[...].astype(f32))
    small_out[7:11, :] = jnp.where(lax.broadcasted_iota(jnp.int32, (4, D), 0) == shard, pre_sum, 0.0)

    def head_grads(at):
        spot = pl.ds(at, 256)
        gheads[spot, :] = dot(branch[spot, :], wo[...], nt).astype(bf16)

    fold_out = Fold(2, both_ways)
    part[2][pl.ds(far, 256), :] = dot(act[pl.ds(far, 256), :], wp[...]).astype(bf16)
    fold_out.start_far()
    part[2][pl.ds(near, 256), :] = dot(act[pl.ds(near, 256), :], wp[...]).astype(bf16)
    fold_out.start_near()
    go_branch.near()
    head_grads(near)
    go_branch.far()
    head_grads(far)
    fold_out.cross()
    sum_one.two_start()
    for h in range(heads):
        q, k, v = (mixed[:, head(h, i)] for i in range(3))
        gh = gheads[:, head(h, 0)]
        gmixed[:, head(h, 2)] = dot(gh, probs[h], tn).T.astype(bf16)

        def scores_grad(i):
            spot = slice(i * 256, i * 256 + 256)
            p = probs[h, spot, :].astype(f32)
            gp = dot(gheads[spot, head(h, 0)], mixed[:, head(h, 2)], nt)
            gs = (p * (gp - jnp.sum(p * gp, axis=-1, keepdims=True))).astype(bf16)
            probs[h, spot, :] = gs
            gmixed[spot, head(h, 0)] = (dot(gs, mixed[:, head(h, 1)]) * scale).astype(bf16)

        for i in range(2):
            scores_grad(i)
        gmixed[:, head(h, 1)] = (dot(q, probs[h], tn).T * scale).astype(bf16)

    grad_columns(parts_two, 0, head_out, branch, hc)
    grad_columns(parts_two, hc, gmixed, nrm, hc)
    sum_two.one_start()
    sum_one.z_start()
    fold = Fold(3, one_way)
    part[3][pl.ds(far, 256), :] = dot(gmixed[pl.ds(far, 256), :], wq[...]).astype(bf16)
    fold.start_far()
    part[3][pl.ds(near, 256), :] = dot(gmixed[pl.ds(near, 256), :], wq[...]).astype(bf16)
    fold.start_near()
    fold.cross()
    mixed_sum = total(gmixed[...].astype(f32))
    spread_out = (lax.broadcasted_iota(jnp.int32, (hc, D), 0) + shard * hc == lax.broadcasted_iota(jnp.int32, (hc, D), 1)).astype(f32)
    for row, lo in ((4, 0), (5, 2 * hc)):
        small_out[row : row + 1, :] = jnp.dot(mixed_sum[:, lo : lo + hc], spread_out, precision=lax.Precision.HIGHEST, preferred_element_type=f32)
    out_ref[...] = ((resid[...] + fold_out.end() + small[11:12, :]) * live).astype(bf16)
    sum_two.one_pass()
    sum_one.back_start()
    sum_two.two_start()
    c_one = fold.end()
    hat = xhat1[...]
    small_out[0:1, :] = total(c_one * hat)
    small_out[1:2, :] = total(c_one)
    small_step()
    dx_ref[...] = gres[...] + norm_grad(hat, r_one, small[0:1, :], c_one)
    sum_one.last_start()
    small_step()
    sum_two.z_start()
    sum_one.last_pass()
    sum_two.back_start()
    small_step()

    def update(u, base, mom, sums):
        count = u.shape[0]
        for k in range(2):
            cols = slice(k * HALF, k * HALF + HALF)
            g = sums[k, base : base + count, :].astype(f32)
            u[:, cols] = (g + momentum_decay * (momentum_decay * mom[:, cols] + g)).astype(bf16)

    n = D // 16
    at = (pl.multiple_of((x * 4 + y) * n, 16), pl.multiple_of((y * 4 + x) * n, 16))

    def gram_rows(m, u, whole):
        for k in range(2):
            cols = slice(k * HALF, k * HALF + HALF)
            if whole:
                piece[m, k] = dot(u[pl.ds(at[k], n), :], u[cols, :], nt)
            else:
                pick = (lax.broadcasted_iota(jnp.int32, (D, n), 0) == lax.broadcasted_iota(jnp.int32, (D, n), 1) + at[k]).astype(f32).astype(bf16)
                piece[m, k] = dot(dot(u[...], pick).astype(bf16), u[:, cols], tn)

    sum_two.last_start()
    sum_one.last_end()
    for load in mom_loads:
        load.wait()
    update(u_fc, 0, wf32, sums_one)
    update(wp, D, wp32, sums_one)
    gram_rows(2, u_fc, True)
    gram_rows(3, wp, False)
    sum_two.last_pass()
    sum_two.last_end()
    update(wo, 0, wo32, sums_two)
    update(uq, hc, momq, sums_two)
    gram_rows(1, wo, False)
    gram_rows(0, uq, False)
    over_z = [partner, device(x, y, 1 - z, par)]
    over_z_next = [device(x, y, z, (sib + 2) % 4), device(x, y, 1 - z, (sib + 2) % 4)]
    orth_factors(place(), sides, sibling, over_z, over_z_next, copy, at, piece, gram_got, halves, gram, gram_low, poly, factor_low, q_all, small_step)
    assert used[0] <= RECVS and len(free) == SENDS


def run_block(x_own, cot, lengths, order, wq, wo, wf, wp, mq, mo, mf, mp, small):
    vm = pl.BlockSpec(memory_space=pltpu.VMEM)
    sm = pl.BlockSpec(memory_space=pltpu.SMEM)
    hbm = pl.BlockSpec(memory_space=pl.ANY)
    rows, wide = x_own.shape[0], wq.shape[0]
    hc = wide // 3
    group = 4 * rows
    vmem = pltpu.VMEM
    return pl.pallas_call(
        block_kernel,
        out_shape=(
            pltpu.VMEM((rows, D), bf16),
            pltpu.VMEM((rows, D), f32),
            pltpu.VMEM((2, 2 * D, HALF), bf16),
            pltpu.VMEM((2, D, HALF), bf16),
            pltpu.VMEM((12, D), f32),
            pltpu.VMEM((4, 3, HALF, HALF), bf16),
            pltpu.VMEM((D, D), bf16),
            *[pltpu.VMEM(w.shape, f32) for w in (wq, wo, wf, wp, wf, wp)],
        ),
        in_specs=[vm, vm, sm, sm] + [hbm] * 8 + [vm],
        out_specs=(vm,) * 13,
        scratch_shapes=[
            vmem((4 * group, D), bf16),
            vmem((group, wide), bf16),
            vmem((hc // HD, group, group), bf16),
            vmem((group, group), f32),
            vmem((group, hc), bf16),
            vmem((4 * group, D), bf16),
            vmem((4, 3, rows, D), bf16),
            vmem((4, rows, D), bf16),
            vmem(wq.shape, bf16),
            vmem(wo.shape, bf16),
            vmem(wf.shape, bf16),
            vmem(wp.shape, bf16),
            vmem((group, D), f32),
            vmem((group, D), bf16),
            vmem((group, D), bf16),
            vmem((group, hc), bf16),
            vmem((group, wide), bf16),
            vmem((rows, D), f32),
            vmem((rows, D), f32),
            vmem((rows, D), f32),
            vmem((rows, D), f32),
            vmem((2, 2 * D, HALF), bf16),
            vmem((2, D, HALF), bf16),
            *sum_scratch(2 * D),
            *sum_scratch(D),
            vmem((12, D), f32),
            vmem((1, wide), f32),
            vmem((1, group), jnp.int32),
            vmem((wide, D), bf16),
            vmem((4, 2, D // 16, HALF), f32),
            vmem((3, 2, D // 16, HALF), f32),
            vmem((2, D, HALF), f32),
            vmem((D, D), f32),
            vmem((D, D), bf16),
            vmem((7, 12, D), f32),
            pltpu.SemaphoreType.DMA((SENDS,)),
            pltpu.SemaphoreType.DMA((RECVS,)),
            pltpu.SemaphoreType.DMA((10,)),
        ],
        compiler_params=pltpu.CompilerParams(collective_id=1, has_side_effects=True, vmem_limit_bytes=40 * 1024 * 1024),
    )(x_own, cot, lengths, order, wq, wo, wf, wp, mq, mo, mf, mp, small)


def finish_kernel(
    sums_one, sums_two, q_all, u_fc, mq, mo, mf, mp, wf, wp, out_in, dx_in, small_sum, small_params, small_first, small_second,
    wq, wo,
    out_ref, dx_ref, gq, go, gf, gp, nq, no, nf, np_, rq, ro, rf, rp, small_grad, first_ref, second_ref, small_new, last_bias,
):
    i = pl.program_id(0)
    nt, tn = ((1,), (1,)), ((0,), (0,))

    @pl.when(i == 0)
    def _():
        out_ref[...] = out_in[...]
        dx_ref[...] = dx_in[...]
        g = small_sum[...]
        small_grad[...] = g
        last_bias[...] = g[11:12, :]
        first = beta_one * small_first[...] + (1.0 - beta_one) * g
        second = beta_two * small_second[...] + (1.0 - beta_two) * g * g
        first_ref[...] = first
        second_ref[...] = second
        first_hat = first / (1.0 - beta_one**STEP)
        second_hat = second / (1.0 - beta_two**STEP)
        small_new[...] = small_params[...] - adam_rate * first_hat / (jnp.sqrt(second_hat) + adam_eps)

    def renew(owner, sums, base, w, m, g_out, w_out, m_out, longest, rate):
        count = g_out.shape[0]
        keep_rate, step_rate = 1.0 - rate * muon_decay, rate * 0.2 * math.sqrt(longest)
        spot = pl.ds(pl.multiple_of(base + i * count, 16), count)
        mine = pl.ds(pl.multiple_of(i * count, 16), count)
        held = mine if w.shape[0] > count else pl.ds(0, count)
        low = []
        for k in range(2):
            cols = slice(k * HALF, k * HALF + HALF)
            g = sums[k, spot, :].astype(f32)
            moved = momentum_decay * m[mine, cols] + g
            g_out[:, cols] = g
            m_out[:, cols] = moved
            low.append((g + momentum_decay * moved).astype(bf16))
        q11, q12, q22 = q_all[owner, 0], q_all[owner, 1], q_all[owner, 2]
        w_out[:, :HALF] = keep_rate * w[held, :HALF] - step_rate * (dot(low[0], q11) + dot(low[1], q12, nt))
        w_out[:, HALF:] = keep_rate * w[held, HALF:] - step_rate * (dot(low[0], q12) + dot(low[1], q22))

    renew(0, sums_two, 192, wq, mq, gq, nq, rq, 3 * D, muon_rate)
    renew(1, sums_two, 0, wo, mo, go, no, ro, D, out_rate)
    renew(3, sums_one, D, wp, mp, gp, np_, rp, FF, muon_rate)
    count = gf.shape[0]
    keep_rate, step_rate = 1.0 - muon_rate * muon_decay, muon_rate * 0.2 * math.sqrt(FF)
    spot = pl.ds(pl.multiple_of(i * count, 16), count)
    for k in range(2):
        cols = slice(k * HALF, k * HALF + HALF)
        g = sums_one[k, spot, :].astype(f32)
        gf[:, cols] = g
        rf[:, cols] = momentum_decay * mf[spot, cols] + g
    half_steps = HALF // count

    @pl.when(i < half_steps)
    def _():
        at = pl.ds(pl.multiple_of(i * count, count), count)
        nf[...] = keep_rate * wf[spot, :] - step_rate * (dot(q_all[2, 0, at, :], u_fc[:HALF, :]) + dot(q_all[2, 1, at, :], u_fc[HALF:, :]))

    @pl.when(i >= half_steps)
    def _():
        at = pl.ds(pl.multiple_of((i - half_steps) * count, count), count)
        nf[...] = keep_rate * wf[spot, :] - step_rate * (dot(q_all[2, 1, :, at], u_fc[:HALF, :], tn) + dot(q_all[2, 2, at, :], u_fc[HALF:, :]))


def finish(kept, small, weights):
    steps = 6
    vm = pl.BlockSpec(memory_space=pltpu.VMEM)

    def tiles(a):
        return pl.BlockSpec((a.shape[0] // steps, a.shape[1]), lambda i: (i, 0))

    def whole(shape):
        return pl.BlockSpec(shape, lambda i: (0, 0))

    like = [jax.ShapeDtypeStruct(w.shape, f32) for w in weights]
    flat = jax.ShapeDtypeStruct((12, D), f32)
    last = jax.ShapeDtypeStruct((1, D), f32)
    block_out, dx = kept[10], kept[11]
    own = [jax.ShapeDtypeStruct(block_out.shape, bf16), jax.ShapeDtypeStruct(dx.shape, f32)]
    return pl.pallas_call(
        finish_kernel,
        grid=(steps,),
        out_shape=(*own, *like, *like, *like, flat, flat, flat, flat, last),
        in_specs=[vm] * 16 + [tiles(w) for w in weights[:2]],
        out_specs=(whole(block_out.shape), whole(dx.shape), *([tiles(w) for w in weights] * 3), *([whole((12, D))] * 4), whole((1, D))),
        compiler_params=pltpu.CompilerParams(vmem_limit_bytes=24 * 1024 * 1024),
    )(*kept, *small, *weights[:2])


def shards(block_input, cotangent, lengths, block_order, w_qkv, w_out, w_fc, w_proj, mom_qkv, mom_out, mom_fc, mom_proj, small_params, small_first, small_second):
    cube = w_qkv.shape

    def turned(a):
        return a.transpose(1, 2, 0).reshape(-1, D)

    def back(a):
        return a.reshape(cube[1], cube[2], D).transpose(2, 0, 1)

    weights = (turned(w_qkv), w_out, w_fc, w_proj)
    moms = (turned(mom_qkv), mom_out, mom_fc, mom_proj)
    block_output, input_grad, sums_one, sums_two, small_sum, factors, u_fc, *held = run_block(block_input, cotangent, lengths, block_order, *weights, *moms, small_params)
    kept = [sums_one, sums_two, factors, u_fc, *held, block_output, input_grad, small_sum]
    kept = [pltpu.with_memory_space_constraint(a, pltpu.VMEM) for a in kept]
    weights = [pltpu.with_memory_space_constraint(a, pltpu.HBM) for a in weights]
    block_output, input_grad, gq, go, gf, gp, nq, no, nf, np_, rq, ro, rf, rp, grad_small, first, second, new_small, last = finish(
        kept, (small_params, small_first, small_second), weights
    )
    return (
        block_output, input_grad, back(gq), go, gf, gp, grad_small, back(nq), no, nf, np_, back(rq), ro, rf, rp, first, second, new_small, last.reshape(D),
    )


def solution(mesh):
    rows = P(("rep", "shard"), None)
    mats = (P(None, None, "shard"), P("shard", None), P(None, "shard"), P("shard", None))
    in_specs = (rows, rows, P("rep"), P("rep", None), *mats, *mats, P(), P(), P())
    out_specs = (rows, rows, *mats, P(), *mats, *mats, P(), P(), P(), P())
    return jax.shard_map(shards, mesh=mesh, in_specs=in_specs, out_specs=out_specs, check_vma=False)
```

profile of v0, /device:TPU:1, one launch (start us, length us, event | category | flops | bytes accessed | tf_op | source)
XLA Modules:
  0.0 155.8 jit_solution(7917410342078401418)
XLA Ops:
  1.3 0.0 copy-start
  1.3 0.0 copy-start.1
  1.3 0.0 copy-start.2
  1.3 141.8 %shard_map.294 = (bf16[128,768]{1,0:T(8,128)(2,1)S(1)}, f32[128,768]{1,0:T(8,128)S(1)}, bf16[2,1536,384]{2,1,0:T(8,128)(2,1)S(1)}, bf16[2,768,384]{2,1,0:T(8,128...) custom-call(bf16[128,768]{1,0:T(8,128)(2,1)} %x_ref.1, ...), custom_call_target="tpu_custom_call" | custom-call | tf_op jit(solution)/shard_map/pallas_call | solution.py:719
  143.1 0.0 copy-done
  143.2 0.0 copy-done.1
  143.2 0.0 copy-done.2
  143.2 12.0 %shard_map.295 = (bf16[128,768]{1,0:T(8,128)(2,1)}, f32[128,768]{1,0:T(8,128)}, f32[576,768]{1,0:T(8,128)}, f32[192,768]{1,0:T(8,128)}, f32[768,768]{1,0:T(8,128...) custom-call(bf16[2,1536,384]{2,1,0:T(8,128)(2,1)S(1)} %get-tuple-ele, ...), custom_call_target="tpu_custom_call" | custom-call | tf_op jit(solution)/shard_map/pallas_call | solution.py:857
  155.2 0.6 reduce
Async XLA Ops:
  1.3 141.8 %copy-start = (f32[12,768]{1,0:T(8,128)S(1)}, f32[12,768]{1,0:T(8,128)}, u32[]{:S(2)}) copy-start(f32[12,768]{1,0:T(8,128)} %small_params.1) | copy-start | bytes 110596
  1.3 141.8 %copy-start.1 = (f32[12,768]{1,0:T(8,128)S(1)}, f32[12,768]{1,0:T(8,128)}, u32[]{:S(2)}) copy-start(f32[12,768]{1,0:T(8,128)} %small_first.1) | copy-start | bytes 110596
  1.3 141.8 %copy-start.2 = (f32[12,768]{1,0:T(8,128)S(1)}, f32[12,768]{1,0:T(8,128)}, u32[]{:S(2)}) copy-start(f32[12,768]{1,0:T(8,128)} %small_second.1) | copy-start | bytes 110596
where the time goes:
time: 156 us
  Pallas kernels  154 us (99%)
    pallas_call x1, Pallas kernels, run_block(): pl.pallas_call(block_kernel, out_shape=(pltpu.VMEM((rows, D), bf16), pltp...  142 us
    pallas_call x1, Pallas kernels, finish(): pl.pallas_call(finish_kernel, grid=(steps,), out_shape=(*own, *like, *lik...  12 us

commit v1 on v0

--- a/solution.py
+++ b/solution.py
@@ -293,24 +293,35 @@
                 gram[spot, :] = g
                 gram_low[later][spot, :] = g.astype(bf16)
 
-        for r in range(blocks):
-            poly_rows(r)
-        for r in range(blocks):
-            update_rows(r)
-    small_step()
+        if k < 3:
+            for r in range(blocks):
+                poly_rows(r)
+            for r in range(blocks):
+                update_rows(r)
+    top, low_part, every = pl.ds(0, HALF // 2), pl.ds(HALF // 2, HALF // 2), pl.ds(0, HALF)
+    cross = []
+
+    def send(way, block, spot):
+        view = q_all.at[shard, block, spot, :]
+        cross.append((copy(view, view, over_z[way]), block, spot))
+
+    for r in range(2):
+        poly_rows(r)
+        update_rows(r)
     q_all[shard, 0] = (halves[0, 0:HALF, :] * inv).astype(bf16)
     q_all[shard, 1] = (halves[1, 0:HALF, :] * inv).astype(bf16)
+    send(0, 1, top)
+    send(1, 1, low_part)
+    send(0, 0, every)
+    poly_rows(2)
+    update_rows(2)
     q_all[shard, 2] = (halves[1, HALF:D, :] * inv).astype(bf16)
-    top, low_part = pl.ds(0, HALF // 2), pl.ds(HALF // 2, HALF // 2)
-    cross = []
-    for k in range(2):
-        for block, spot in ((1, (top, low_part)[k]), (2 * k, pl.ds(0, HALF))):
-            view = q_all.at[shard, block, spot, :]
-            cross.append((copy(view, view, over_z[k]), block, spot))
+    send(1, 2, every)
     near = copy(q_all.at[shard], q_all.at[shard], sibling)
+    small_step()
     away = (shard + 2) % 4
     onward = []
-    for c, block, spot in (cross[0], cross[2], cross[1], cross[3]):
+    for c, block, spot in cross:
         c.wait_recv()
         view = q_all.at[away, block, spot, :]
         onward.append(copy(view, view, sibling))

time: 156 us -> 154 us (0.987)
  Pallas kernels: 154 us -> 152 us
    pallas_call x1, Pallas kernels: 142 us -> 140 us  [run_block(): pl.pallas_call(block_kernel, out_shape=(pltpu.VMEM((rows, D), bf16), pltp...]
where the time goes in v1:
time: 154 us
  Pallas kernels  152 us (99%)
    pallas_call x1, Pallas kernels, run_block(): pl.pallas_call(block_kernel, out_shape=(pltpu.VMEM((rows, D), bf16), pltp...  140 us
    pallas_call x1, Pallas kernels, finish(): pl.pallas_call(finish_kernel, grid=(steps,), out_shape=(*own, *like, *lik...  12 us

profile of v1, /device:TPU:1, one launch (start us, length us, event | category | flops | bytes accessed | tf_op | source)
XLA Modules:
  0.0 154.2 jit_solution(13634614787520248193)
XLA Ops:
  1.3 0.0 copy-start
  1.3 0.0 copy-start.1
  1.3 0.0 copy-start.2
  1.3 140.2 %shard_map.294 = (bf16[128,768]{1,0:T(8,128)(2,1)S(1)}, f32[128,768]{1,0:T(8,128)S(1)}, bf16[2,1536,384]{2,1,0:T(8,128)(2,1)S(1)}, bf16[2,768,384]{2,1,0:T(8,128...) custom-call(bf16[128,768]{1,0:T(8,128)(2,1)} %x_ref.1, ...), custom_call_target="tpu_custom_call" | custom-call | tf_op jit(solution)/shard_map/pallas_call | solution.py:730
  141.5 0.0 copy-done
  141.6 0.0 copy-done.1
  141.6 0.0 copy-done.2
  141.6 12.0 %shard_map.295 = (bf16[128,768]{1,0:T(8,128)(2,1)}, f32[128,768]{1,0:T(8,128)}, f32[576,768]{1,0:T(8,128)}, f32[192,768]{1,0:T(8,128)}, f32[768,768]{1,0:T(8,128...) custom-call(bf16[2,1536,384]{2,1,0:T(8,128)(2,1)S(1)} %get-tuple-ele, ...), custom_call_target="tpu_custom_call" | custom-call | tf_op jit(solution)/shard_map/pallas_call | solution.py:868
  153.6 0.6 reduce
Async XLA Ops:
  1.3 140.2 %copy-start = (f32[12,768]{1,0:T(8,128)S(1)}, f32[12,768]{1,0:T(8,128)}, u32[]{:S(2)}) copy-start(f32[12,768]{1,0:T(8,128)} %small_params.1) | copy-start | bytes 110596
  1.3 140.2 %copy-start.1 = (f32[12,768]{1,0:T(8,128)S(1)}, f32[12,768]{1,0:T(8,128)}, u32[]{:S(2)}) copy-start(f32[12,768]{1,0:T(8,128)} %small_first.1) | copy-start | bytes 110596
  1.3 140.2 %copy-start.2 = (f32[12,768]{1,0:T(8,128)S(1)}, f32[12,768]{1,0:T(8,128)}, u32[]{:S(2)}) copy-start(f32[12,768]{1,0:T(8,128)} %small_second.1) | copy-start | bytes 110596
